TPU v7x, 32 devices: a whole 2x2x4 slice. The times are simulated.
32 devices in a mesh: leaf: 2 (over y), row: 2 (over x), col: 8 (over z, core).
Axes of the slice: x: 2, y: 2, z: 4, core: 2. Of those that a mesh axis runs over, the one named last changes fastest.
Arguments:
- front_window: float32 [49152, 2048], P(('leaf', 'row'), 'col'), parts along dimension 0, may hold values from -8 to 785
- children: float32 [65536, 2048], P(('leaf', 'row', 'col')), parts along dimension 0, may hold values from -1 to 1
- row_map: int32 [4, 128], P('leaf'), parts along dimension 0, may hold values from 0 to 191, as said below
- col_map: int32 [4, 16], P('leaf'), parts along dimension 0, may hold values from 0 to 15, as said below
Outputs:
- factored: float32 [49152, 2048], P(('leaf', 'row'), 'col'), parts along dimension 0
There are 2 independent parts, one for each index of `leaf`. A program takes and returns all parts, laid end to end along the dimension named above; each array names one. Nothing has to cross between parts.
Inputs may be any that keep to these rules, and one draw needn't show every extreme that they name: `row_map`: for each sibling, its entries are distinct; each aligned run of 128 of its row blocks names exactly 64 blocks in each range of 96 consecutive parent blocks. `col_map`: each sibling's row is a permutation of the 16 window blocks.
All inputs are finite; a program needn't handle non-finite values.
Results may differ from a plain program's by a relative error of at most 0.000088.
Values sent between devices are 32-bit elements; how exact they have to be, the bound alone decides.
A program may use at most 192 MiB of HBM per device.

v0:
```python
import jax
import jax.numpy as jnp
from jax import lax
from jax.sharding import PartitionSpec as P

BLK = 128
PANEL = 256


def broadcast(value, axis, source):
    kept = jnp.where(lax.axis_index(axis) == source, value, 0).astype(value.dtype)
    return lax.psum(kept, axis)


def body(front_window, children, row_map, col_map):
    row_count = lax.axis_size("row")
    col_count = lax.axis_size("col")
    row_index = lax.axis_index("row")
    col_index = lax.axis_index("col")
    rows_here, cols_here = front_window.shape
    child_rows = children.shape[0]
    window_blocks = children.shape[1] // BLK
    sibling = row_index // (row_count // 2)
    chosen_cols = lax.dynamic_index_in_dim(col_map, sibling, 0, keepdims=False)
    inverse_cols = jnp.argsort(chosen_cols)
    spread = jnp.take(children.reshape(child_rows, window_blocks, BLK), inverse_cols, axis=1)
    spread = spread.reshape(child_rows, col_count, cols_here)
    quarter = lax.all_to_all(spread, "col", split_axis=1, concat_axis=0, tiled=True)
    quarter = quarter.reshape(col_count * child_rows, cols_here)
    quarter_blocks = quarter.shape[0] // BLK
    capacity = quarter_blocks // row_count
    parent_blocks = rows_here // BLK
    source_maps = row_map.reshape(row_count, quarter_blocks)
    owners = source_maps // parent_blocks
    ordering = jnp.argsort(owners, axis=1, stable=True)
    own_order = lax.dynamic_index_in_dim(ordering, row_index, 0, keepdims=False)
    outgoing = jnp.take(quarter.reshape(quarter_blocks, BLK, cols_here), own_order, axis=0)
    outgoing = outgoing.reshape(row_count, capacity * BLK, cols_here)
    incoming = lax.all_to_all(outgoing, "row", split_axis=0, concat_axis=0, tiled=True)
    chosen = lax.dynamic_slice_in_dim(ordering, row_index * capacity, capacity, axis=1)
    targets = (jnp.take_along_axis(source_maps, chosen, axis=1) % parent_blocks).reshape(-1)
    selector = (targets[:, None] == jnp.arange(parent_blocks, dtype=jnp.int32)[None, :]).astype(
        jnp.float32
    )
    added = jnp.einsum(
        "sp,sk->pk",
        selector,
        incoming.reshape(row_count * capacity, BLK * cols_here),
        precision=lax.Precision.HIGHEST,
    )
    assembled = front_window + added.reshape(rows_here, cols_here)
    identity = jnp.eye(PANEL, dtype=jnp.float32)
    global_rows = row_index * rows_here + jnp.arange(rows_here, dtype=jnp.int32)
    panel_rows = broadcast(assembled, "col", 0)
    diagonal_block = broadcast(panel_rows[:PANEL], "row", 0)
    factor = jnp.linalg.cholesky(diagonal_block)
    inverse = jax.scipy.linalg.solve_triangular(factor, identity, lower=True)
    solved = jnp.dot(panel_rows, inverse.T, precision=lax.Precision.HIGHEST)
    leading = jnp.where(row_index == 0, factor, solved[:PANEL])
    lower_panel = jnp.concatenate([leading, solved[PANEL:]], axis=0)
    owner_row = col_index * cols_here // rows_here
    start = jnp.clip(col_index * cols_here - row_index * rows_here, 0, rows_here - cols_here)
    piece = lax.dynamic_slice_in_dim(lower_panel, start, cols_here, 0)
    matching = broadcast(piece, "row", owner_row)
    update = jnp.dot(lower_panel, matching.T, precision=lax.Precision.HIGHEST)
    global_cols = col_index * cols_here + jnp.arange(cols_here, dtype=jnp.int32)
    inside = (global_rows >= PANEL)[:, None] & (global_cols >= PANEL)[None, :]
    result = jnp.where(inside, assembled - update, assembled)
    return jnp.where((global_cols < PANEL)[None, :], lower_panel, result)


def solution(mesh):
    placed = (
        P(("leaf", "row"), "col"),
        P(("leaf", "row", "col"), None),
        P("leaf", None),
        P("leaf", None),
    )
    return jax.shard_map(
        body, mesh=mesh, in_specs=placed, out_specs=P(("leaf", "row"), "col"), check_vma=False
    )
```

profile of v0, /device:TPU:0, one launch (start us, length us, event | category | flops | bytes accessed | tf_op | source)
XLA Modules:
  0.0 1209.6 jit_solution(6401520857214902791)
XLA Ops:
  8.5 17.6 %copy.29 = f32[2048,2048]{0,1:T(8,128)} copy(f32[2048,2048]{1,0:T(8,128)} %param.5) | data formatting | bytes 33554432 | tf_op args[1]
  26.1 17.6 %copy.30 = f32[2048,16,128]{2,0,1:T(8,128)} copy(f32[2048,16,128]{0,2,1:T(8,128)} %bitcast.65) | data formatting | bytes 33554432 | tf_op jit(solution)/shard_map/reshape | solution.py:26
  43.7 13.8 %gather_fusion = f32[16,2048,128]{2,1,0:T(8,128)} fusion(f32[2048,16,128]{2,0,1:T(8,128)} %copy.30, s32[1024]{0:T(1024)S(1)} %pad_clamp_fusion.1), kind=kCustom, calls=%fused_computation | custom fusion | bytes 33554496 | tf_op jit(solution)/shard_map/jit(_take)/gather | solution.py:26
  57.5 17.6 %copy.31 = f32[2048,16,128]{0,2,1:T(8,128)} copy(f32[2048,16,128]{2,0,1:T(8,128)} %bitcast.63) | data formatting | bytes 33554432 | tf_op jit(solution)/shard_map/jit(_take)/gather | solution.py:26
  100.2 356.8 %all-to-all-done = f32[2048,8,256]{0,2,1:T(8,128)} async-done(((f32[2048,8,256]{0,2,1:T(8,128)}), f32[2048,8,256]{0,2,1:T(8,128)}, u32[]{:S(2)}, u32[]{:S(2)}) %all-to-all-start) | async-done | bytes 16777248 | tf_op jit(solution)/shard_map/all_to_all | solution.py:28
  457.1 16.4 %copy.32 = f32[8,2048,1,256]{3,1,0,2:T(8,128)} copy(f32[8,2048,1,256]{1,3,0,2:T(8,128)} %bitcast.7) | data formatting | bytes 33554432 | tf_op jit(solution)/shard_map/all_to_all | solution.py:28
  473.5 15.6 %gather_fusion.1 = f32[128,128,256]{2,1,0:T(8,128)} fusion(f32[128,128,256]{2,1,0:T(8,128)} %bitcast.64, s32[1024]{0:T(1024)S(1)} %pad_clamp_fusion), kind=kCustom, calls=%fused_computation.1 | custom fusion | bytes 33554944 | tf_op jit(solution)/shard_map/jit(_take)/gather | solution.py:37
  489.1 12.2 %bitcast_select_fusion = f32[2,8192,256]{2,1,0:T(8,128)} fusion(pred[2,8192]{1,0:T(4,128)(4,1)S(1)} %bitcast.66, f32[2,8192,256]{2,1,0:T(8,128)} %bitcast.61), kind=kLoop, calls=%fused_computation.8 | loop fusion | flops 4194304 | bytes 33570816 | tf_op jit(solution)/shard_map/jit(_take)/select_n | solution.py:37
  511.4 12.6 %copy.33 = f32[12288,256]{0,1:T(8,128)} copy(f32[12288,256]{1,0:T(8,128)} %param.4) | data formatting | bytes 25165824 | tf_op args[0]
  525.9 167.8 %all-to-all-done.1 = f32[2,8192,256]{2,1,0:T(8,128)} async-done(((f32[2,8192,256]{2,1,0:T(8,128)}), f32[2,8192,256]{2,1,0:T(8,128)}, u32[]{:S(2)}, u32[]{:S(2)}) %all-to-all-start.1) | async-done | bytes 16777248 | tf_op jit(solution)/shard_map/all_to_all | solution.py:39
  693.7 18.2 %reshape.123 = f32[128,32768]{1,0:T(8,128)} reshape(f32[2,8192,256]{2,1,0:T(8,128)} %all-to-all-done.1) | data formatting | bytes 33554432 | tf_op jit(solution)/shard_map/reshape | solution.py:48
  712.0 14.2 %fusion.17 = f32[96,32768]{1,0:T(8,128)} fusion(f32[128,32768]{1,0:T(8,128)} %reshape.123, s32[128]{0:T(128)S(1)} %and_select_fusion), kind=kOutput, calls=%fused_computation.46 | convolution fusion | flops 4831850496 | bytes 29360640 | tf_op jit(solution)/shard_map/sp,sk->pk/dot_general | solution.py:45
  726.2 13.6 %reshape.124 = f32[12288,256]{1,0:T(8,128)} reshape(f32[96,32768]{1,0:T(8,128)} %fusion.17) | data formatting | bytes 25165824 | tf_op jit(solution)/shard_map/reshape | solution.py:51
  739.8 12.6 %copy.34 = f32[12288,256]{0,1:T(8,128)} copy(f32[12288,256]{1,0:T(8,128)} %reshape.124) | data formatting | bytes 25165824 | tf_op jit(solution)/shard_map/reshape | solution.py:51
  752.4 18.5 %broadcast_select_fusion = (f32[12288,256]{0,1:T(8,128)}, f32[12288,256]{0,1:T(8,128)}) fusion(pred[]{:T(512)S(6)} %eq.31, f32[12288,256]{0,1:T(8,128)} %copy.33, f32[12288,256]{0,1:T(8,128)} %copy.34), kind=kLoop, calls=%fused_computation.13 | loop fusion | flops 6291456 | bytes 50331648 | tf_op jit(solution)/shard_map/jit(_where)/select_n | solution.py:11
  771.0 253.3 %all-reduce.5.cloned.1.call-done = f32[12288,256]{0,1:T(8,128)} async-done(((f32[12288,256]{0,1:T(8,128)}), f32[12288,256]{0,1:T(8,128)}) %all-reduce.5.cloned.1.call-update) | async-done | bytes 12582928 | tf_op jit(solution)/shard_map/psum | solution.py:12
  1026.7 23.4 %all-reduce.7.cloned.1.call-done = f32[256,256]{0,1:T(8,128)} async-done(((f32[256,256]{0,1:T(8,128)}), f32[256,256]{0,1:T(8,128)}) %all-reduce.7.cloned.1.call-update) | async-done | bytes 262160 | tf_op jit(solution)/shard_map/psum | solution.py:12
  1052.3 11.7 cholesky.49
  1074.3 11.7 cholesky.103
  1092.8 19.7 %custom-call.16 = f32[2,128,128]{1,2,0:T(8,128)S(1)} custom-call(f32[2,128,128]{2,1,0:T(8,128)S(1)} %get-tuple-element.16), custom_call_target="InvertDiagBlocksLowerTriangular" | custom-call | tf_op jit(solution)/shard_map/jit(_solve_triangular)/triangular_solve | solution.py:57
  1113.3 14.1 %fusion.3 = f32[12288,256]{0,1:T(8,128)S(1)} fusion(f32[12288,256]{0,1:T(8,128)} %all-reduce.5.cloned.1.call-done, f32[128,256]{1,0:T(8,128)S(1)} %fusion.13, f32[128,256]{1,0:T(8,128)S(1)} %fusion.10), kind=kOutput, calls=%fused_computation.19 | convolution fusion | flops 9663741952 | bytes 25427968 | tf_op jit(solution)/shard_map/dot_general | solution.py:58
  1143.8 23.4 %all-reduce.9.cloned.1.call-done = f32[256,256]{0,1:T(8,128)} async-done(((f32[256,256]{0,1:T(8,128)}), f32[256,256]{0,1:T(8,128)}) %all-reduce.9.cloned.1.call-update) | async-done | bytes 262160 | tf_op jit(solution)/shard_map/psum | solution.py:12
  1167.2 23.0 %fusion = f32[12288,256]{0,1:T(8,128)} fusion(f32[12288,256]{0,1:T(8,128)} %get-tuple-element.38, f32[256,256]{0,1:T(8,128)} %all-reduce.9.cloned.1.call-done, f32[256,256]{0,1:T(8,128)S(1)} %slice_select_fusion, f32[12032,256]{0,1:T(8,128)} %slice.79, pred[256]{0:T(512)(128)(4,1)S(1)} %get-tuple-element.44, pred[12288]{0:T(1024)(128)(4,1)S(1)} %add_compare_fusion, ...), kind=kOutput, calls=%fused_computation.10 | convolution fusion | flops 9682550784 | bytes 38023680 | tf_op jit(solution)/shard_map/dot_general | solution.py:65
  1190.2 12.6 %copy.43 = f32[12288,256]{1,0:T(8,128)} copy(f32[12288,256]{0,1:T(8,128)} %fusion) | data formatting | bytes 25165824 | tf_op jit(solution)/shard_map/jit(_where)/select_n | solution.py:69
  (87 shorter events, 80.5 us)
Async XLA Ops:
  6.5 0.7 copy-start
  86.8 6.5 copy-start.2
  86.8 370.3 %all-to-all-start = ((f32[2048,8,256]{0,2,1:T(8,128)}), f32[2048,8,256]{0,2,1:T(8,128)}, u32[]{:S(2)}, u32[]{:S(2)}) async-start(f32[2048,8,256]{0,2,1:T(8,128)} %bitcast_select_fusion.1), calls=%async_computation | async-start | bytes 33554432 | tf_op jit(solution)/shard_map/all_to_all | solution.py:28
  93.2 5.4 sort.37.cloned.1.call-start
  501.3 192.4 %all-to-all-start.1 = ((f32[2,8192,256]{2,1,0:T(8,128)}), f32[2,8192,256]{2,1,0:T(8,128)}, u32[]{:S(2)}, u32[]{:S(2)}) async-start(f32[2,8192,256]{2,1,0:T(8,128)} %bitcast_select_fusion), calls=%async_computation.1 | async-start | bytes 33554432 | tf_op jit(solution)/shard_map/all_to_all | solution.py:39
  511.0 513.4 %all-reduce.5.cloned.1.call-start = ((), (), s32[]{:S(2)}) async-start(), calls=%async_computation.2 | async-start | bytes 25165824 | tf_op jit(solution)/shard_map/psum | solution.py:12
  511.4 12.6 %copy-start.4 = (s32[2,128]{1,0:T(2,128)S(1)}, s32[2,128]{1,0:T(2,128)}, u32[]{:S(2)}) copy-start(s32[2,128]{1,0:T(2,128)} %get-tuple-element.7) | copy-start | bytes 3076
  771.0 279.2 %all-reduce.7.cloned.1.call-start = ((), (), s32[]{:S(2)}) async-start(), calls=%async_computation.3 | async-start | bytes 524288 | tf_op jit(solution)/shard_map/psum | solution.py:12
  1026.1 141.2 %all-reduce.9.cloned.1.call-start = ((), (), s32[]{:S(2)}) async-start(), calls=%async_computation.4 | async-start | bytes 524288 | tf_op jit(solution)/shard_map/psum | solution.py:12
  1127.5 4.8 copy-start.3
  1167.2 35.6 %copy-start.1 = (s32[2,16]{1,0:T(2,128)S(1)}, s32[2,16]{1,0:T(2,128)}, u32[]{:S(2)}) copy-start(s32[2,16]{1,0:T(2,128)} %param.7) | copy-start | bytes 388
Sparse Core Ops, SparseCore 0:
  96.3 2.0 sort.39.cloned.1.call-done
  771.1 253.2 all-reduce.4
  1026.7 23.3 all-reduce.6
  1143.9 23.2 all-reduce.8
  (1 shorter events, 0.0 us)
where the time goes:
time: 1220 us; the launch traced here: 1210 us
  waiting for transfers between devices  825 us (68%)
  local copies, waits for them, and re-layouts  197 us (16%)
  other arithmetic  103 us (8%)
  matrix products  52.6 us (4%)
  starting transfers between devices  17.1 us (1%)
  between operations  14.9 us (1%)
    all_to_all x1, waiting for transfers between devices, body(): lax.all_to_all(spread, 'col', split_axis=1, concat_axis=0, tiled=True)  357 us
    psum x3, waiting for transfers between devices, broadcast(): return lax.psum(kept, axis)  300 us
    all_to_all x1, waiting for transfers between devices, body(): lax.all_to_all(outgoing, 'row', split_axis=0, concat_axis=0, tiled=True)  168 us
    unnamed x15, local copies, waits for them, and re-layouts  35.8 us
    another operation x6, other arithmetic, body(): factor = jnp.linalg.cholesky(diagonal_block)  34 us
    gather x2, local copies, waits for them, and re-layouts, body(): jnp.take(children.reshape(child_rows, window_blocks, BLK), inverse_cols,...  31.4 us
    reshape x2, local copies, waits for them, and re-layouts, body(): assembled = front_window + added.reshape(rows_here, cols_here)  26.2 us
  transfers between devices with their start and end apart: 5, of which 5 were waited for; matrix products, arithmetic and copies ran while one was open for 1% of the time, Pallas kernels for 0%

commit v1 on v0

--- a/solution.py
+++ b/solution.py
@@ -25,7 +25,19 @@
     inverse_cols = jnp.argsort(chosen_cols)
     spread = jnp.take(children.reshape(child_rows, window_blocks, BLK), inverse_cols, axis=1)
     spread = spread.reshape(child_rows, col_count, cols_here)
-    quarter = lax.all_to_all(spread, "col", split_axis=1, concat_axis=0, tiled=True)
+    ways, here = (lax.axis_size("col"), lax.axis_index("col"))
+    width = spread.shape[1] // ways
+    shape = list(spread.shape)
+    shape[1] = width
+    height = shape[0]
+    shape[0] = height * ways
+    full = jnp.zeros(shape, spread.dtype)
+    for mask in range(ways):
+        part = lax.dynamic_slice_in_dim(spread, (here ^ mask) * width, width, axis=1)
+        if mask:
+            part = lax.ppermute(part, "col", [(d, d ^ mask) for d in range(ways)])
+        full = lax.dynamic_update_slice_in_dim(full, part, (here ^ mask) * height, axis=0)
+    quarter = full
     quarter = quarter.reshape(col_count * child_rows, cols_here)
     quarter_blocks = quarter.shape[0] // BLK
     capacity = quarter_blocks // row_count

time: 1220 us -> 1220 us (level)
  waiting for transfers between devices: 825 us -> 773 us
  local copies, waits for them, and re-layouts: 197 us -> 230 us
  starting transfers between devices: 17.1 us -> 31.6 us
    all_to_all x1 -> x0, waiting for transfers between devices: 357 us -> none  [body(): lax.all_to_all(spread, 'col', split_axis=1, concat_axis=0, tiled=True)]
    ppermute x0 -> x7, waiting for transfers between devices: none -> 224 us  [body(): part = lax.ppermute(part, 'col', [(d, d ^ mask) for d in range(ways)])]
    psum x3, waiting for transfers between devices: 300 us -> 409 us  [broadcast(): return lax.psum(kept, axis)]
    all_to_all x1, waiting for transfers between devices: 168 us -> 139 us  [body(): lax.all_to_all(outgoing, 'row', split_axis=0, concat_axis=0, tiled=True)]
    ppermute x0 -> x7, local copies, waits for them, and re-layouts: none -> 18.4 us  [body(): part = lax.ppermute(part, 'col', [(d, d ^ mask) for d in range(ways)])]
    all_to_all x1 -> x0, local copies, waits for them, and re-layouts: 16.4 us -> none  [body(): lax.all_to_all(spread, 'col', split_axis=1, concat_axis=0, tiled=True)]
    dynamic_update_slice x0 -> x8, local copies, waits for them, and re-layouts: none -> 15 us  [body(): lax.dynamic_update_slice_in_dim(full, part, (here ^ mask) * height, axis=0)]
    dynamic_slice x0 -> x2, local copies, waits for them, and re-layouts: none -> 12.7 us  [body(): lax.dynamic_slice_in_dim(spread, (here ^ mask) * width, width, axis=1)]
  transfers between devices with their start and end apart: 5 -> 11, of which waited for: 5 -> 8; matrix products, arithmetic and copies ran while one was open for 1% -> 5% of each run, Pallas kernels for 0% -> 0%
where the time goes in v1:
time: 1220 us; the launch traced here: 1210 us
  waiting for transfers between devices  773 us (63%)
  local copies, waits for them, and re-layouts  230 us (19%)
  other arithmetic  103 us (8%)
  matrix products  52.7 us (4%)
  starting transfers between devices  31.6 us (3%)
  between operations  15.2 us (1%)
    psum x3, waiting for transfers between devices, broadcast(): return lax.psum(kept, axis)  409 us
    ppermute x7, waiting for transfers between devices, body(): part = lax.ppermute(part, 'col', [(d, d ^ mask) for d in range(ways)])  224 us
    all_to_all x1, waiting for transfers between devices, body(): lax.all_to_all(outgoing, 'row', split_axis=0, concat_axis=0, tiled=True)  139 us
    unnamed x25, local copies, waits for them, and re-layouts  37.1 us
    another operation x6, other arithmetic, body(): factor = jnp.linalg.cholesky(diagonal_block)  34 us
    gather x2, local copies, waits for them, and re-layouts, body(): jnp.take(children.reshape(child_rows, window_blocks, BLK), inverse_cols,...  31.4 us
    reshape x2, local copies, waits for them, and re-layouts, body(): assembled = front_window + added.reshape(rows_here, cols_here)  26.3 us
  transfers between devices with their start and end apart: 11, of which 8 were waited for; matrix products, arithmetic and copies ran while one was open for 5% of the time, Pallas kernels for 0%

profile of v1, /device:TPU:0, one launch (start us, length us, event | category | flops | bytes accessed | tf_op | source)
XLA Modules:
  0.0 1205.1 jit_solution(18062723308142882122)
XLA Ops:
  8.5 17.6 %copy.44 = f32[2048,2048]{0,1:T(8,128)} copy(f32[2048,2048]{1,0:T(8,128)} %param.5) | data formatting | bytes 33554432 | tf_op args[1]
  26.1 17.6 %copy.45 = f32[2048,16,128]{2,0,1:T(8,128)} copy(f32[2048,16,128]{0,2,1:T(8,128)} %bitcast.61) | data formatting | bytes 33554432 | tf_op jit(solution)/shard_map/reshape | solution.py:26
  43.7 13.8 %gather_fusion = f32[16,2048,128]{2,1,0:T(8,128)} fusion(f32[2048,16,128]{2,0,1:T(8,128)} %copy.45, s32[1024]{0:T(1024)S(1)} %pad_clamp_fusion.1), kind=kCustom, calls=%fused_computation | custom fusion | bytes 33554496 | tf_op jit(solution)/shard_map/jit(_take)/gather | solution.py:26
  57.5 17.6 %copy.46 = f32[2048,16,128]{0,2,1:T(8,128)} copy(f32[2048,16,128]{2,0,1:T(8,128)} %bitcast.60) | data formatting | bytes 33554432 | tf_op jit(solution)/shard_map/jit(_take)/gather | solution.py:26
  119.9 117.2 %collective-permute-done.1 = f32[2048,1,256]{0,2,1:T(8,128)} collective-permute-done((f32[2048,1,256]{0,2,1:T(8,128)}, f32[2048,1,256]{0,2,1:T(8,128)}, u32[]{:S(2)}, u32[]{:S(2)}) %collective-permute-start.1) | collective-permute-done | bytes 2097184 | tf_op jit(solution)/shard_map/ppermute | solution.py:38
  243.2 38.3 %collective-permute-done.2 = f32[2048,1,256]{0,2,1:T(8,128)} collective-permute-done((f32[2048,1,256]{0,2,1:T(8,128)}, f32[2048,1,256]{0,2,1:T(8,128)}, u32[]{:S(2)}, u32[]{:S(2)}) %collective-permute-start.2) | collective-permute-done | bytes 2097184 | tf_op jit(solution)/shard_map/ppermute | solution.py:38
  290.3 39.7 %collective-permute-done.5 = f32[2048,1,256]{0,2,1:T(8,128)} collective-permute-done((f32[2048,1,256]{0,2,1:T(8,128)}, f32[2048,1,256]{0,2,1:T(8,128)}, u32[]{:S(2)}, u32[]{:S(2)}) %collective-permute-start.5) | collective-permute-done | bytes 2097184 | tf_op jit(solution)/shard_map/ppermute | solution.py:38
  345.0 29.0 %collective-permute-done.6 = f32[2048,1,256]{0,2,1:T(8,128)} collective-permute-done((f32[2048,1,256]{0,2,1:T(8,128)}, f32[2048,1,256]{0,2,1:T(8,128)}, u32[]{:S(2)}, u32[]{:S(2)}) %collective-permute-start.6) | collective-permute-done | bytes 2097184 | tf_op jit(solution)/shard_map/ppermute | solution.py:38
  377.4 15.6 %gather_fusion.1 = f32[128,128,256]{2,1,0:T(8,128)} fusion(f32[128,128,256]{2,1,0:T(8,128)} %bitcast.6, s32[1024]{0:T(1024)S(1)} %pad_clamp_fusion), kind=kCustom, calls=%fused_computation.1 | custom fusion | bytes 33554944 | tf_op jit(solution)/shard_map/jit(_take)/gather | solution.py:49
  393.0 12.2 %bitcast_select_fusion = f32[2,8192,256]{2,1,0:T(8,128)} fusion(pred[2,8192]{1,0:T(4,128)(4,1)S(1)} %bitcast.62, f32[2,8192,256]{2,1,0:T(8,128)} %bitcast.58), kind=kLoop, calls=%fused_computation.8 | loop fusion | flops 4194304 | bytes 33570816 | tf_op jit(solution)/shard_map/jit(_take)/select_n | solution.py:49
  426.7 12.6 %copy.55 = f32[12288,256]{0,1:T(8,128)} copy(f32[12288,256]{1,0:T(8,128)} %param.4) | data formatting | bytes 25165824 | tf_op args[0]
  441.3 139.0 %all-to-all-done = f32[2,8192,256]{2,1,0:T(8,128)} async-done(((f32[2,8192,256]{2,1,0:T(8,128)}), f32[2,8192,256]{2,1,0:T(8,128)}, u32[]{:S(2)}, u32[]{:S(2)}) %all-to-all-start) | async-done | bytes 16777248 | tf_op jit(solution)/shard_map/all_to_all | solution.py:51
  580.3 18.2 %reshape.122 = f32[128,32768]{1,0:T(8,128)} reshape(f32[2,8192,256]{2,1,0:T(8,128)} %all-to-all-done) | data formatting | bytes 33554432 | tf_op jit(solution)/shard_map/reshape | solution.py:60
  598.5 14.1 %fusion.17 = f32[96,32768]{1,0:T(8,128)} fusion(f32[128,32768]{1,0:T(8,128)} %reshape.122, s32[128]{0:T(128)S(1)} %and_select_fusion), kind=kOutput, calls=%fused_computation.46 | convolution fusion | flops 4831850496 | bytes 29360640 | tf_op jit(solution)/shard_map/sp,sk->pk/dot_general | solution.py:57
  612.6 13.6 %reshape.123 = f32[12288,256]{1,0:T(8,128)} reshape(f32[96,32768]{1,0:T(8,128)} %fusion.17) | data formatting | bytes 25165824 | tf_op jit(solution)/shard_map/reshape | solution.py:63
  626.3 12.6 %copy.56 = f32[12288,256]{0,1:T(8,128)} copy(f32[12288,256]{1,0:T(8,128)} %reshape.123) | data formatting | bytes 25165824 | tf_op jit(solution)/shard_map/reshape | solution.py:63
  638.9 18.5 %broadcast_select_fusion = (f32[12288,256]{0,1:T(8,128)}, f32[12288,256]{0,1:T(8,128)}) fusion(pred[]{:T(512)S(6)} %eq.31, f32[12288,256]{0,1:T(8,128)} %copy.55, f32[12288,256]{0,1:T(8,128)} %copy.56), kind=kLoop, calls=%fused_computation.13 | loop fusion | flops 6291456 | bytes 50331648 | tf_op jit(solution)/shard_map/jit(_where)/select_n | solution.py:11
  657.5 362.1 %all-reduce.5.cloned.1.call-done = f32[12288,256]{0,1:T(8,128)} async-done(((f32[12288,256]{0,1:T(8,128)}), f32[12288,256]{0,1:T(8,128)}) %all-reduce.5.cloned.1.call-update) | async-done | bytes 12582928 | tf_op jit(solution)/shard_map/psum | solution.py:12
  1021.5 23.9 %all-reduce.7.cloned.1.call-done = f32[256,256]{0,1:T(8,128)} async-done(((f32[256,256]{0,1:T(8,128)}), f32[256,256]{0,1:T(8,128)}) %all-reduce.7.cloned.1.call-update) | async-done | bytes 262160 | tf_op jit(solution)/shard_map/psum | solution.py:12
  1088.0 19.7 %custom-call.16 = f32[2,128,128]{1,2,0:T(8,128)S(1)} custom-call(f32[2,128,128]{2,1,0:T(8,128)S(1)} %get-tuple-element.16), custom_call_target="InvertDiagBlocksLowerTriangular" | custom-call | tf_op jit(solution)/shard_map/jit(_solve_triangular)/triangular_solve | solution.py:69
  1108.6 14.1 %fusion.3 = f32[12288,256]{0,1:T(8,128)S(1)} fusion(f32[12288,256]{0,1:T(8,128)} %all-reduce.5.cloned.1.call-done, f32[128,256]{1,0:T(8,128)S(1)} %fusion.13, f32[128,256]{1,0:T(8,128)S(1)} %fusion.10), kind=kOutput, calls=%fused_computation.19 | convolution fusion | flops 9663741952 | bytes 25427968 | tf_op jit(solution)/shard_map/dot_general | solution.py:70
  1139.1 23.4 %all-reduce.9.cloned.1.call-done = f32[256,256]{0,1:T(8,128)} async-done(((f32[256,256]{0,1:T(8,128)}), f32[256,256]{0,1:T(8,128)}) %all-reduce.9.cloned.1.call-update) | async-done | bytes 262160 | tf_op jit(solution)/shard_map/psum | solution.py:12
  1162.5 23.1 %fusion = f32[12288,256]{0,1:T(8,128)} fusion(f32[12288,256]{0,1:T(8,128)} %get-tuple-element.42, f32[256,256]{0,1:T(8,128)} %all-reduce.9.cloned.1.call-done, f32[256,256]{0,1:T(8,128)S(1)} %slice_select_fusion, f32[12032,256]{0,1:T(8,128)} %slice.79, pred[256]{0:T(512)(128)(4,1)S(1)} %get-tuple-element.56, pred[12288]{0:T(1024)(128)(4,1)S(1)} %add_compare_fusion, ...), kind=kOutput, calls=%fused_computation.10 | convolution fusion | flops 9682550784 | bytes 38023680 | tf_op jit(solution)/shard_map/dot_general | solution.py:77
  1185.5 12.6 %copy.65 = f32[12288,256]{1,0:T(8,128)} copy(f32[12288,256]{0,1:T(8,128)} %fusion) | data formatting | bytes 25165824 | tf_op jit(solution)/shard_map/jit(_where)/select_n | solution.py:81
  (126 shorter events, 167.7 us)
Async XLA Ops:
  6.5 0.7 copy-start
  6.5 112.7 %sort.37.cloned.1.call-start = ((), (), s32[]{:S(2)}) async-start(), calls=%async_computation.4 | async-start | bytes 6176 | tf_op jit(solution)/shard_map/jit(argsort)/sort | solution.py:47
  86.9 21.8 %copy-start.2 = (s32[2,128]{1,0:T(2,128)S(1)}, s32[2,128]{1,0:T(2,128)}, u32[]{:S(2)}) copy-start(s32[2,128]{1,0:T(2,128)} %param.6) | copy-start | bytes 3076
  97.8 6.0 collective-permute-start
  98.3 138.9 %collective-permute-start.1 = (f32[2048,1,256]{0,2,1:T(8,128)}, f32[2048,1,256]{0,2,1:T(8,128)}, u32[]{:S(2)}, u32[]{:S(2)}) collective-permute-start(f32[2048,1,256]{0,2,1:T(8,128)} %get-tuple-element.50), channel_id=1, source_target_pairs={{0,2},{1,3},{2,0},{3,1},{4,6},{5,7},{6,4},{7,5},{8,10},{9,11},{10,... | collective-permute-start | bytes 6291464 | tf_op jit(solution)/shard_map/ppermute | solution.py:38
  100.9 180.6 %collective-permute-start.2 = (f32[2048,1,256]{0,2,1:T(8,128)}, f32[2048,1,256]{0,2,1:T(8,128)}, u32[]{:S(2)}, u32[]{:S(2)}) collective-permute-start(f32[2048,1,256]{0,2,1:T(8,128)} %get-tuple-element.49), channel_id=1, source_target_pairs={{0,3},{1,2},{2,1},{3,0},{4,7},{5,6},{6,5},{7,4},{8,11},{9,10},{10,... | collective-permute-start | bytes 6291464 | tf_op jit(solution)/shard_map/ppermute | solution.py:38
  101.0 183.5 %collective-permute-start.3 = (f32[2048,1,256]{0,2,1:T(8,128)}, f32[2048,1,256]{0,2,1:T(8,128)}, u32[]{:S(2)}, u32[]{:S(2)}) collective-permute-start(f32[2048,1,256]{0,2,1:T(8,128)} %get-tuple-element.48), channel_id=1, source_target_pairs={{0,4},{1,5},{2,6},{3,7},{4,0},{5,1},{6,2},{7,3},{8,12},{9,13},{10,... | collective-permute-start | bytes 6291464 | tf_op jit(solution)/shard_map/ppermute | solution.py:38
  103.8 183.6 %collective-permute-start.4 = (f32[2048,1,256]{0,2,1:T(8,128)}, f32[2048,1,256]{0,2,1:T(8,128)}, u32[]{:S(2)}, u32[]{:S(2)}) collective-permute-start(f32[2048,1,256]{0,2,1:T(8,128)} %get-tuple-element.47), channel_id=1, source_target_pairs={{0,5},{1,4},{2,7},{3,6},{4,1},{5,0},{6,3},{7,2},{8,13},{9,12},{10,... | collective-permute-start | bytes 6291464 | tf_op jit(solution)/shard_map/ppermute | solution.py:38
  103.8 1.3 copy-start.8
  105.1 224.9 %collective-permute-start.5 = (f32[2048,1,256]{0,2,1:T(8,128)}, f32[2048,1,256]{0,2,1:T(8,128)}, u32[]{:S(2)}, u32[]{:S(2)}) collective-permute-start(f32[2048,1,256]{0,2,1:T(8,128)} %get-tuple-element.46), channel_id=1, source_target_pairs={{0,6},{1,7},{2,4},{3,5},{4,2},{5,3},{6,0},{7,1},{8,14},{9,15},{10,... | collective-permute-start | bytes 6291464 | tf_op jit(solution)/shard_map/ppermute | solution.py:38
  111.7 6.0 copy-start.7
  237.2 136.9 %collective-permute-start.6 = (f32[2048,1,256]{0,2,1:T(8,128)}, f32[2048,1,256]{0,2,1:T(8,128)}, u32[]{:S(2)}, u32[]{:S(2)}) collective-permute-start(f32[2048,1,256]{0,2,1:T(8,128)} %get-tuple-element.45), channel_id=1, source_target_pairs={{0,7},{1,6},{2,5},{3,4},{4,3},{5,2},{6,1},{7,0},{8,15},{9,14},{10,... | collective-permute-start | bytes 6291464 | tf_op jit(solution)/shard_map/ppermute | solution.py:38
  332.9 7.7 copy-start.4
  332.9 9.2 copy-start.5
  332.9 10.7 copy-start.6
  405.2 175.0 %all-to-all-start = ((f32[2,8192,256]{2,1,0:T(8,128)}), f32[2,8192,256]{2,1,0:T(8,128)}, u32[]{:S(2)}, u32[]{:S(2)}) async-start(f32[2,8192,256]{2,1,0:T(8,128)} %bitcast_select_fusion), calls=%async_computation | async-start | bytes 33554432 | tf_op jit(solution)/shard_map/all_to_all | solution.py:51
  414.9 604.7 %all-reduce.5.cloned.1.call-start = ((), (), s32[]{:S(2)}) async-start(), calls=%async_computation.1 | async-start | bytes 25165824 | tf_op jit(solution)/shard_map/psum | solution.py:12
  426.7 12.6 %copy-start.9 = (s32[2,128]{1,0:T(2,128)S(1)}, s32[2,128]{1,0:T(2,128)}, u32[]{:S(2)}) copy-start(s32[2,128]{1,0:T(2,128)} %get-tuple-element.7) | copy-start | bytes 3076
  657.5 387.9 %all-reduce.7.cloned.1.call-start = ((), (), s32[]{:S(2)}) async-start(), calls=%async_computation.2 | async-start | bytes 524288 | tf_op jit(solution)/shard_map/psum | solution.py:12
  1021.3 141.1 %all-reduce.9.cloned.1.call-start = ((), (), s32[]{:S(2)}) async-start(), calls=%async_computation.3 | async-start | bytes 524288 | tf_op jit(solution)/shard_map/psum | solution.py:12
  1122.7 4.8 copy-start.3
  1162.5 35.7 %copy-start.1 = (s32[2,16]{1,0:T(2,128)S(1)}, s32[2,16]{1,0:T(2,128)}, u32[]{:S(2)}) copy-start(s32[2,16]{1,0:T(2,128)} %param.7) | copy-start | bytes 388
Sparse Core Ops, SparseCore 0:
  110.0 2.0 sort.39.cloned.1.call-done
  657.6 362.0 all-reduce.4
  1021.9 23.3 all-reduce.6
  1139.1 23.2 all-reduce.8
  (1 shorter events, 0.0 us)
